TPU v7x, 128 devices: a whole 4x4x4 slice. The times are simulated.
128 devices in a mesh: pool: 2 (over core), dev: 64 (over x, y, z).
Axes of the slice: x: 4, y: 4, z: 4, core: 2. Of those that a mesh axis runs over, the one named last changes fastest.
Arguments:
- queries: bfloat16 [4, 1024, 8, 576], P(None, 'dev'), may hold values from -9 to 9
- new_latent: bfloat16 [4, 1024, 576], P(None, 'dev'), may hold values from -4 to 4
- cache: bfloat16 [1024, 128, 576], P('dev'), may hold values from -4 to 4
- lengths: int32 [1024], P('dev'), may hold values from 4 to 128, as said below
- hidden_in: bfloat16 [4, 1024, 2048], P(None, 'dev'), may hold values from -4 to 4
- norm_gain: float32 [2048], replicated, may hold values from 0.1 to 1.9
- uv_weight: bfloat16 [8, 512, 128], replicated, may hold values from -0.25 to 0.25
- out_weight: bfloat16 [1024, 2048], replicated, may hold values from -0.1875 to 0.1875
- expert_ids: int32 [4, 1024, 6], P(None, 'dev'), may hold values from 0 to 63, as said below
- gate_weight: bfloat16 [4, 1024, 6], P(None, 'dev'), may hold values from 0.049804688 to 0.59765625
- capacity: int32 [64], replicated, may hold values from 2 to 3
- gate_up: bfloat16 [64, 2048, 2816], P('dev'), may hold values from -0.125 to 0.125
- down: bfloat16 [64, 1408, 2048], P('dev'), may hold values from -0.15625 to 0.15625
Outputs:
- output: bfloat16 [4, 1024, 2048], P(None, 'dev', 'pool')
Inputs may be any that keep to these rules, and one draw needn't show every extreme that they name: `expert_ids`: each row names 6 different experts; at each step one expert is named by the first 3 requests of every aligned block of 8 requests, and its capacity is 3. `lengths`: every device holds a request of length 128.
All inputs are finite; a program needn't handle non-finite values.
Results may differ from a plain program's by a relative error of at most 0.01.
Values may be sent and summed in bfloat16 or wider, within the bound.
No kernel may reach another device: no remote copies, remote signals or barrier semaphores. Data moves between devices by JAX's collectives and lax.ppermute only.
A program may use at most 128 MiB of HBM per device.

v0:
```python
import functools

import jax
import jax.numpy as jnp
from jax import lax
from jax.experimental import pallas as pl
from jax.experimental.pallas import tpu as pltpu
from jax.sharding import PartitionSpec as P

LAT = 512
ROPE = 64
QKNOPE = 128
CAP = 3
MICRO = 2
CHUNKS = 1
ROWS = 24
F32 = jnp.float32
BF16 = jnp.bfloat16
MIB = 1024 * 1024


def iota(shape, dim):
    return lax.broadcasted_iota(jnp.int32, shape, dim)


def dot(a, b, contract=((1,), (0,))):
    return lax.dot_general(a, b, (contract, ((), ())), preferred_element_type=F32)


def attend_kernel(
    pool_ref, len_ref, q_ref, nl_ref, cache_ref, hid_ref, gain_ref, uv_ref, ow_hbm, ids_ref, gw_ref, cap_ref,
    *rest,
):
    outs = rest[: 3 * CHUNKS]
    mixed_ref, lat_sc, ow_sc, ow_sem = rest[3 * CHUNKS :]
    fetch = pltpu.make_async_copy(ow_hbm, ow_sc, ow_sem)
    fetch.start()
    pool = pool_ref[0]
    steps, reqs, heads, width = q_ref.shape
    ctx = cache_ref.shape[1]
    model = hid_ref.shape[2]
    experts = cap_ref.shape[1]
    tokens = steps * reqs
    per_req = steps * heads
    scale = (QKNOPE + ROPE) ** (-0.5)

    def mine(ref):
        wide = ref[...].astype(F32) if ref.dtype != jnp.int32 else ref[...]
        part = jnp.where(pool == 0, wide[:, :reqs], wide[:, reqs:])
        return part.reshape(tokens, wide.shape[2])

    fresh = mine(nl_ref).astype(BF16)
    q_rows = [q_ref[:, r].astype(F32).reshape(per_req, width).astype(BF16) for r in range(reqs)]
    position = iota((per_req, ctx), 1)
    old = []
    for r in range(reqs):
        s = dot(q_rows[r], cache_ref[r], ((1,), (1,))) * scale
        old.append(jnp.where(position < len_ref[pool * reqs + r], s, -jnp.inf))
    old = jnp.concatenate(old, axis=0)
    new = dot(jnp.concatenate(q_rows, axis=0), fresh, ((1,), (1,))) * scale
    row = iota(new.shape, 0)
    col = iota(new.shape, 1)
    valid = (row // per_req == col % reqs) & (col // reqs <= (row // heads) % steps)
    new = jnp.where(valid, new, -jnp.inf)
    top = jnp.maximum(jnp.max(old, axis=1, keepdims=True), jnp.max(new, axis=1, keepdims=True))
    old = jnp.exp(old - top)
    new = jnp.exp(new - top)
    total = jnp.sum(old, axis=1, keepdims=True) + jnp.sum(new, axis=1, keepdims=True)
    old = old.astype(BF16)
    latent = jnp.concatenate(
        [dot(old[r * per_req : (r + 1) * per_req], cache_ref[r, :, :LAT]) for r in range(reqs)], axis=0
    )
    latent = latent + dot(new.astype(BF16), fresh[:, :LAT])
    latent = latent / total
    for i in range(lat_sc.shape[0]):
        lat_sc[i] = latent[:, i * 128 : (i + 1) * 128]
    head_out = []
    for h in range(heads):
        rows = [
            jnp.concatenate(
                [lat_sc[i, pl.ds(s * heads + h, reqs, stride=per_req), :] for i in range(lat_sc.shape[0])],
                axis=1,
            )
            for s in range(steps)
        ]
        lat_h = jnp.concatenate(rows, axis=0).astype(BF16)
        head_out.append(dot(lat_h, uv_ref[h]).astype(BF16))
    head_out = jnp.concatenate(head_out, axis=1)

    ids = mine(ids_ref)
    gates = mine(gw_ref)
    lane = iota((tokens, experts), 1)
    named = jnp.zeros((tokens, experts), F32)
    gate = jnp.zeros((tokens, experts), F32)
    for k in range(ids.shape[1]):
        hit = ids[:, k : k + 1] == lane
        named = named + hit.astype(F32)
        gate = gate + jnp.where(hit, gates[:, k : k + 1], 0.0)
    a, b = iota((tokens, tokens), 0), iota((tokens, tokens), 1)
    earlier = ((a // reqs == b // reqs) & (b < a)).astype(BF16)
    before = dot(earlier, named.astype(BF16))
    kept = (named > 0) & (before < cap_ref[...].astype(F32))
    per_chunk = tokens // CHUNKS
    slots = CAP * steps // CHUNKS
    parts = ROWS // slots
    step_in_chunk = (iota((tokens, experts), 0) % per_chunk) // reqs
    slot = jnp.where(kept, step_in_chunk.astype(F32) * CAP + before, -100.0)

    fetch.wait()
    mixed = mine(hid_ref) + dot(head_out, ow_sc[...])
    mixed_ref[...] = mixed
    normed = (
        mixed * lax.rsqrt(jnp.mean(mixed * mixed, axis=1, keepdims=True) + 1e-06) * gain_ref[...]
    ).astype(BF16)

    lanes = parts * per_chunk
    spread = (iota((per_chunk, lanes), 1) % per_chunk == iota((per_chunk, lanes), 0)).astype(BF16)
    offset = (iota((experts, lanes), 1) // per_chunk * slots).astype(F32)
    wide = model // parts
    for c in range(CHUNKS):
        x_ref, at_ref, gate_ref = outs[3 * c : 3 * c + 3]
        rows = slice(c * per_chunk, (c + 1) * per_chunk)
        at = dot(slot[rows].astype(BF16), spread, ((0,), (0,))) + offset
        at_ref[...] = at
        gate_ref[...] = dot(gate[rows].astype(BF16), spread, ((0,), (0,)))
        stacked = jnp.concatenate(
            [normed[rows, i * wide : (i + 1) * wide] for i in range(parts)], axis=0
        )
        some = 16
        for e in range(0, experts, some):
            place = (iota((some, ROWS, lanes), 1).astype(F32) == at[e : e + some][:, None, :]).astype(F32)
            place = place.reshape(some * ROWS, lanes).astype(BF16)
            x_ref[e * ROWS : (e + some) * ROWS, :] = dot(place, stacked).astype(BF16)


def attend(pool, lengths, queries, new_latent, cache, hidden_in, gain, uv, ow, ids, gates, capacity):
    steps, demand, heads, width = queries.shape
    reqs = demand // MICRO
    model = hidden_in.shape[2]
    experts = capacity.shape[1]
    tokens = steps * reqs
    per_chunk = tokens // CHUNKS
    parts = ROWS // (CAP * steps // CHUNKS)
    lanes = parts * per_chunk
    outs = []
    for _ in range(CHUNKS):
        outs += [
            jax.ShapeDtypeStruct((experts * ROWS, model // parts), BF16),
            jax.ShapeDtypeStruct((experts, lanes), F32),
            jax.ShapeDtypeStruct((experts, lanes), F32),
        ]
    outs.append(jax.ShapeDtypeStruct((tokens, model), F32))
    full = lambda a: pl.BlockSpec(a.shape, lambda i, p: (0,) * a.ndim)
    return pl.pallas_call(
        attend_kernel,
        out_shape=outs,
        grid_spec=pltpu.PrefetchScalarGridSpec(
            num_scalar_prefetch=1,
            grid=(1,),
            in_specs=[
                pl.BlockSpec(memory_space=pltpu.SMEM),
                pl.BlockSpec((steps, reqs, heads, width), lambda i, p: (0, p[0], 0, 0)),
                full(new_latent),
                pl.BlockSpec((reqs,) + cache.shape[1:], lambda i, p: (p[0], 0, 0)),
                full(hidden_in),
                full(gain),
                full(uv),
                pl.BlockSpec(memory_space=pl.ANY),
                full(ids),
                full(gates),
                full(capacity),
            ],
            out_specs=[full(o) for o in outs],
            scratch_shapes=[
                pltpu.VMEM((LAT // 128, tokens * heads, 128), F32),
                pltpu.VMEM(ow.shape, BF16),
                pltpu.SemaphoreType.DMA,
            ],
        ),
        compiler_params=pltpu.CompilerParams(vmem_limit_bytes=48 * MIB),
        name="attend",
    )(pool, lengths, queries, new_latent, cache, hidden_in, gain, uv, ow, ids, gates, capacity)


GROUP = 8


def order_matrix(slots):
    n = GROUP * ROWS
    o, i = iota((n, n), 0), iota((n, n), 1)
    per_part = GROUP * slots
    source = (o % per_part) // slots
    want = source * ROWS + (o // per_part) * slots + o % slots
    return (want == i).astype(BF16)


def serve_kernel(x_ref, gate_ref, up_ref, down_hbm, y_ref, rows_sc, act_sc, down_sc, y_sc, sem):
    step = pl.program_id(0)
    n_rows, model = rows_sc.shape
    wide = x_ref.shape[1]
    parts = model // wide
    slots = ROWS // parts
    n = GROUP * ROWS
    per_part = GROUP * slots
    groups = x_ref.shape[0] // n
    fetch = pltpu.make_async_copy(down_hbm, down_sc, sem)

    @pl.when(step == 0)
    def _():
        fetch.start()
        order = order_matrix(slots)
        for g in range(groups):
            got = dot(order, x_ref[g * n : (g + 1) * n, :]).astype(BF16)
            for i in range(parts):
                rows_sc[g * per_part : (g + 1) * per_part, i * wide : (i + 1) * wide] = got[
                    i * per_part : (i + 1) * per_part
                ]

    cols = gate_ref.shape[2]
    weight = jnp.concatenate([gate_ref[0], up_ref[0]], axis=1)
    both = dot(rows_sc[...], weight)
    gate = both[:, :cols]
    act = gate / (1.0 + jnp.exp(-gate)) * both[:, cols:]
    act_sc[step] = act.astype(BF16)

    @pl.when(step == pl.num_programs(0) - 1)
    def _():
        fetch.wait()
        act_all = jnp.concatenate([act_sc[i] for i in range(act_sc.shape[0])], axis=1)
        block = 256
        for i in range(model // block):
            y_sc[:, i * block : (i + 1) * block] = dot(
                act_all, down_sc[:, i * block : (i + 1) * block]
            ).astype(BF16)
        order = order_matrix(slots)
        for g in range(groups):
            piece = jnp.concatenate(
                [
                    y_sc[g * per_part : (g + 1) * per_part, i * wide : (i + 1) * wide]
                    for i in range(parts)
                ],
                axis=0,
            )
            y_ref[g * n : (g + 1) * n, :] = dot(order, piece, ((0,), (0,))).astype(BF16)


def serve(x, gate_up, down):
    n_in, wide = x.shape
    _, model, twice = gate_up.shape
    hidden = twice // 2
    cols = 128
    count = hidden // cols
    n_rows = n_in * wide // model
    return pl.pallas_call(
        serve_kernel,
        out_shape=jax.ShapeDtypeStruct((n_in, wide), BF16),
        grid=(count,),
        in_specs=[
            pl.BlockSpec((n_in, wide), lambda i: (0, 0)),
            pl.BlockSpec((1, model, cols), lambda i: (0, 0, i)),
            pl.BlockSpec((1, model, cols), lambda i: (0, 0, i + count)),
            pl.BlockSpec(memory_space=pl.ANY),
        ],
        out_specs=pl.BlockSpec((n_in, wide), lambda i: (0, 0)),
        scratch_shapes=[
            pltpu.VMEM((n_rows, model), BF16),
            pltpu.VMEM((count, n_rows, cols), BF16),
            pltpu.VMEM(down.shape[1:], BF16),
            pltpu.VMEM((n_rows, model), BF16),
            pltpu.SemaphoreType.DMA,
        ],
        compiler_params=pltpu.CompilerParams(vmem_limit_bytes=48 * MIB),
        name="serve",
    )(x, gate_up, gate_up, down[0])


def combine_kernel(pool_ref, at_ref, gate_ref, y_ref, mixed_ref, keep_ref, give_ref):
    experts, lanes = at_ref.shape
    tokens, model = mixed_ref.shape
    parts = lanes // tokens
    wide = model // parts
    some = 16
    acc = jnp.zeros((lanes, wide), F32)
    for e in range(0, experts, some):
        hit = iota((some, ROWS, lanes), 1).astype(F32) == at_ref[e : e + some][:, None, :]
        weight = jnp.where(hit, gate_ref[e : e + some][:, None, :], 0.0)
        weight = weight.reshape(some * ROWS, lanes).astype(BF16)
        acc = acc + dot(weight, y_ref[e * ROWS : (e + some) * ROWS, :], ((0,), (0,)))
    moe = jnp.concatenate([acc[i * tokens : (i + 1) * tokens] for i in range(parts)], axis=1)
    out = (mixed_ref[...] + moe)
    first, second = out[:, : model // 2], out[:, model // 2 :]
    lower = pool_ref[0] == 0
    keep_ref[...] = jnp.where(lower, first, second).astype(BF16)
    give_ref[...] = jnp.where(lower, second, first).astype(BF16)


def combine(pool, at, gate, y, mixed, chunk):
    tokens = mixed.shape[0] // CHUNKS
    model = mixed.shape[1]
    full = lambda a: pl.BlockSpec(a.shape, lambda i, p: (0,) * a.ndim)
    half = jax.ShapeDtypeStruct((tokens, model // 2), BF16)
    return pl.pallas_call(
        combine_kernel,
        out_shape=[half, half],
        grid_spec=pltpu.PrefetchScalarGridSpec(
            num_scalar_prefetch=1,
            grid=(1,),
            in_specs=[full(at), full(gate), full(y), pl.BlockSpec((tokens, model), lambda i, p: (chunk, 0))],
            out_specs=[full(half), full(half)],
        ),
        compiler_params=pltpu.CompilerParams(vmem_limit_bytes=48 * MIB),
        name="combine",
    )(pool, at, gate, y, mixed)


def body(
    queries,
    new_latent,
    cache,
    lengths,
    hidden_in,
    norm_gain,
    uv_weight,
    out_weight,
    expert_ids,
    gate_weight,
    capacity,
    gate_up,
    down,
):
    steps, demand = queries.shape[:2]
    reqs = demand // MICRO
    model = hidden_in.shape[2]
    pool = lax.axis_index("pool")
    pool_arr = jnp.full((1,), pool, jnp.int32)
    found = attend(
        pool_arr, lengths, queries, new_latent, cache, hidden_in, norm_gain[None, :], uv_weight, out_weight,
        expert_ids, gate_weight, capacity[None, :],
    )
    mixed = found[-1]
    trade = functools.partial(
        lax.all_to_all, axis_name="dev", split_axis=0, concat_axis=0, tiled=True
    )
    arrived = [trade(found[3 * c]) for c in range(CHUNKS)]
    returned = [trade(serve(x, gate_up, down)) for x in arrived]
    halves = []
    for c in range(CHUNKS):
        keep, give = combine(pool_arr, found[3 * c + 1], found[3 * c + 2], returned[c], mixed, c)
        got = lax.ppermute(give, "pool", [(0, 1), (1, 0)])
        keep = keep.reshape(steps // CHUNKS, reqs, model // 2)
        got = got.reshape(steps // CHUNKS, reqs, model // 2)
        halves.append(
            jnp.where(
                pool == 0,
                jnp.concatenate([keep, got], axis=1),
                jnp.concatenate([got, keep], axis=1),
            )
        )
    return jnp.concatenate(halves, axis=0)


def solution(mesh):
    in_specs = (
        P(None, "dev", None, None),
        P(None, "dev", None),
        P("dev", None, None),
        P("dev"),
        P(None, "dev", None),
        P(),
        P(),
        P(),
        P(None, "dev", None),
        P(None, "dev", None),
        P(),
        P("dev", None, None),
        P("dev", None, None),
    )
    out_specs = P(None, "dev", "pool")
    return jax.shard_map(body, mesh=mesh, in_specs=in_specs, out_specs=out_specs, check_vma=False)
```

profile of v0, /device:TPU:1, one launch (start us, length us, event | category | flops | bytes accessed | tf_op | source)
XLA Modules:
  0.0 141.2 jit_solution(2827644037978167621)
XLA Ops:
  0.0 0.0 copy-start.8
  0.0 0.0 copy-start.1
  0.0 0.0 copy-start.2
  0.0 3.2 %copy.14.cache_ref = bf16[16,128,576]{2,1,0:T(8,128)(2,1)S(1)} copy(bf16[16,128,576]{1,2,0:T(8,128)(2,1)} %param.15) | data formatting | bytes 4718592 | tf_op args[2]
  3.2 0.0 copy-done.8
  3.2 0.7 copy.15.ids_ref
  3.9 0.8 copy.16.gw_ref
  4.7 0.0 copy-done.1
  4.7 0.0 copy-done.2
  4.7 0.0 copy-start
  4.7 1.2 copy-done
  5.9 0.0 copy-start.3
  6.0 0.8 copy-done.3
  6.7 0.0 copy-start.4
  6.7 0.9 copy-done.4
  7.6 0.0 copy-start.5
  7.6 0.7 copy-done.5
  8.3 0.0 copy-start.6
  8.3 0.7 copy-done.6
  8.9 0.0 copy-start.7
  8.9 0.7 copy-done.7
  9.6 7.6 %attend.1 = (bf16[1536,1024]{1,0:T(8,128)(2,1)}, f32[64,64]{1,0:T(8,128)S(1)}, f32[64,64]{1,0:T(8,128)S(1)}, f32[32,2048]{1,0:T(8,128)S(1)}) custom-call(s32[1]{0:T(128)} %bitcast.pool_ref, s32[16]{0:T(128)S(1)} %copy-done.6, bf16[4,16,8,576]{3,2,1,0:T(8,128)(2,1)S(1)} %copy-done.1, bf16[4,16,576]{2,1,0:T(8,128)(2,1)S(1)} %copy-done.4, ...), custom_call_target="tpu_custom_call" | custom-call | tf_op jit(solution)/shard_map/attend/pallas_call | solution.py:154
  17.2 51.2 %all_to_all.22 = bf16[64,24,1024]{2,1,0:T(8,128)(2,1)} all-to-all(bf16[64,24,1024]{2,1,0:T(8,128)(2,1)} %bitcast.17), channel_id=1, replica_groups=mesh['pool'=2,'dev'=64] {'dev'}, dimensions={0} | all-to-all | bytes 6291456 | tf_op jit(solution)/shard_map/all_to_all | solution.py:344
  68.4 21.6 %serve.1 = bf16[1536,1024]{1,0:T(8,128)(2,1)S(1)} custom-call(bf16[1536,1024]{1,0:T(8,128)(2,1)} %bitcast.15, bf16[1,2048,2816]{2,1,0:T(8,128)(2,1)} %up_ref.1, bf16[1,2048,2816]{2,1,0:T(8,128)(2,1)} %up_ref.1, bf16[1408,2048]{1,0:T(8,128)(2,1)} %bitcast.16), custom_call_target="tpu_custom_call" | custom-call | tf_op jit(solution)/shard_map/serve/pallas_call | solution.py:254
  90.0 46.0 %all_to_all.23 = bf16[64,24,1024]{2,1,0:T(8,128)(2,1)S(1)} all-to-all(bf16[64,24,1024]{2,1,0:T(8,128)(2,1)S(1)} %bitcast.10), channel_id=1, replica_groups=mesh['pool'=2,'dev'=64] {'dev'}, dimensions={0} | all-to-all | bytes 6291456 | tf_op jit(solution)/shard_map/all_to_all | solution.py:345
  136.0 0.7 combine.1
  136.7 2.9 %collective-permute-start = (bf16[32,1024]{1,0:T(8,128)(2,1)S(1)}, bf16[32,1024]{1,0:T(8,128)(2,1)S(1)}, u32[]{:S(2)}, u32[]{:S(2)}) collective-permute-start(bf16[32,1024]{1,0:T(8,128)(2,1)S(1)} %get-tuple-element.16), channel_id=1, source_target_pairs={{0,64},{64,0},{1,65},{65,1},{2,66},{66,2},{3,67},{67,3},{4,68},{68... | collective-permute-start | bytes 196616 | tf_op jit(solution)/shard_map/ppermute | solution.py:349
  139.6 0.9 collective-permute-done
  140.5 0.7 maximum_select_fusion
Async XLA Ops:
  0.0 3.2 %copy-start.8 = (s32[4,16,6]{1,0,2:T(4,128)S(1)}, s32[4,16,6]{1,0,2:T(4,128)}, u32[]{:S(2)}) copy-start(s32[4,16,6]{1,0,2:T(4,128)} %param.21) | copy-start | bytes 4612
  0.0 4.7 %copy-start.1 = (bf16[4,16,8,576]{3,2,1,0:T(8,128)(2,1)S(1)}, bf16[4,16,8,576]{3,2,1,0:T(8,128)(2,1)}, u32[]{:S(2)}) copy-start(bf16[4,16,8,576]{3,2,1,0:T(8,128)(2,1)} %q_ref.1) | copy-start | bytes 1769476
  0.0 4.7 %copy-start.2 = (bf16[4,16,2048]{2,1,0:T(8,128)(2,1)S(1)}, bf16[4,16,2048]{2,1,0:T(8,128)(2,1)}, u32[]{:S(2)}) copy-start(bf16[4,16,2048]{2,1,0:T(8,128)(2,1)} %hid_ref.1) | copy-start | bytes 786436
  4.7 1.2 copy-start
  5.9 0.8 copy-start.3
  6.7 0.9 copy-start.4
  7.6 0.7 copy-start.5
  8.3 0.7 copy-start.6
  8.9 0.7 copy-start.7
  136.7 3.8 %collective-permute-start = (bf16[32,1024]{1,0:T(8,128)(2,1)S(1)}, bf16[32,1024]{1,0:T(8,128)(2,1)S(1)}, u32[]{:S(2)}, u32[]{:S(2)}) collective-permute-start(bf16[32,1024]{1,0:T(8,128)(2,1)S(1)} %get-tuple-element.16), channel_id=1, source_target_pairs={{0,64},{64,0},{1,65},{65,1},{2,66},{66,2},{3,67},{67,3},{4,68},{68... | collective-permute-start | bytes 196616 | tf_op jit(solution)/shard_map/ppermute | solution.py:349
where the time goes:
time: 142 us; the launch traced here: 141 us
  blocking collectives  97.1 us (68%)
  Pallas kernels  29.9 us (21%)
  local copies, waits for them, and re-layouts  9.56 us (7%)
  starting transfers between devices  2.9 us (2%)
    all_to_all x1, blocking collectives, body(): arrived = [trade(found[3 * c]) for c in range(CHUNKS)]  51.2 us
    all_to_all x1, blocking collectives, body(): returned = [trade(serve(x, gate_up, down)) for x in arrived]  46 us
    pallas_call x1, Pallas kernels, serve(): pl.pallas_call(serve_kernel, out_shape=jax.ShapeDtypeStruct((n_in, wide),...  21.6 us
    unnamed x21, local copies, waits for them, and re-layouts  9.56 us
    pallas_call x1, Pallas kernels, attend(): pl.pallas_call(attend_kernel, out_shape=outs, grid_spec=pltpu.PrefetchSca...  7.61 us
    ppermute x1, starting transfers between devices, body(): got = lax.ppermute(give, 'pool', [(0, 1), (1, 0)])  2.9 us
  transfers between devices with their start and end apart: 1, of which 1 were waited for; matrix products, arithmetic and copies ran while one was open for 0% of the time, Pallas kernels for 0%

commit v1 on v0

v1 whole, which is shorter than its diff:
```python
import functools

import jax
import jax.numpy as jnp
from jax import lax
from jax.experimental import pallas as pl
from jax.experimental.pallas import tpu as pltpu
from jax.sharding import PartitionSpec as P

LAT = 512
ROPE = 64
QKNOPE = 128
CAP = 3
MICRO = 2
ROWS = 24
F32 = jnp.float32
BF16 = jnp.bfloat16
MIB = 1024 * 1024
SERVE_MIB = 40


def iota(shape, dim):
    return lax.broadcasted_iota(jnp.int32, shape, dim)


def dot(a, b, contract=((1,), (0,))):
    return lax.dot_general(a, b, (contract, ((), ())), preferred_element_type=F32)


def attend_kernel(
    pool_ref, len_hbm, q_hbm, nl_hbm, cache_hbm, hid_hbm, gain_hbm, uv_hbm, ow_hbm, ids_hbm, gw_hbm, cap_hbm,
    x_ref, at_ref, gate_ref, mixed_ref,
    len_sc, q_sc, nl_sc, cache_sc, hid_sc, gain_sc, uv_sc, ow_sc, ids_sc, gw_sc, cap_sc, lat_sc, sem,
):
    pool = pool_ref[0]
    steps, reqs, heads, width = q_sc.shape
    ctx = cache_sc.shape[2]
    model = hid_sc.shape[2]
    experts = cap_sc.shape[1]
    tokens = steps * reqs
    per_req = steps * heads
    scale = (QKNOPE + ROPE) ** (-0.5)

    half = pl.ds(pool * reqs, reqs)
    moves = {}
    for i, (name, src, dst) in enumerate((
        ("len", len_hbm, len_sc),
        ("q", q_hbm.at[:, half], q_sc),
        ("nl", nl_hbm, nl_sc),
        ("cache", cache_hbm.at[half], cache_sc),
        ("ids", ids_hbm, ids_sc),
        ("gw", gw_hbm, gw_sc),
        ("cap", cap_hbm, cap_sc),
        ("uv", uv_hbm, uv_sc),
        ("hid", hid_hbm, hid_sc),
        ("gain", gain_hbm, gain_sc),
        ("ow", ow_hbm, ow_sc),
    )):
        moves[name] = pltpu.make_async_copy(src, dst, sem.at[i])
        moves[name].start()

    def mine(ref):
        wide = ref[...].astype(F32)
        part = jnp.where(pool == 0, wide[:, :reqs], wide[:, reqs:])
        return part.reshape(tokens, wide.shape[2])

    for name in ("len", "q", "nl", "ids", "gw", "cap"):
        moves[name].wait()
    demand = ids_sc.shape[2]
    cap_row = cap_sc[...].astype(F32)
    diagonal = iota((experts, experts), 0) == iota((experts, experts), 1)
    cap = jnp.sum(jnp.where(diagonal, cap_row, 0.0), axis=1, keepdims=True)
    ids = ids_sc[...]
    gates = gw_sc[...].astype(F32)
    mark = iota((experts, demand), 0)
    a, b = iota((demand, demand), 0), iota((demand, demand), 1)
    earlier = ((a // reqs == b // reqs) & (a < b)).astype(BF16)
    slots = CAP * steps
    parts = ROWS // slots
    lanes = parts * tokens
    row, lane = iota((demand, lanes), 0), iota((demand, lanes), 1)
    at = (iota((experts, lanes), 1) // tokens * slots).astype(F32)
    gate_of = jnp.zeros((experts, lanes), F32)
    for s in range(steps):
        named = jnp.zeros((experts, demand), F32)
        gate = jnp.zeros((experts, demand), F32)
        for k in range(ids.shape[0]):
            hit = ids[k, s : s + 1] == mark
            named = named + hit.astype(F32)
            gate = gate + jnp.where(hit, gates[k, s : s + 1], 0.0)
        before = dot(named.astype(BF16), earlier)
        slot = jnp.where((named > 0) & (before < cap), before + s * CAP, -100.0)
        spread = ((lane % tokens == s * reqs + row % reqs) & (row // reqs == pool)).astype(BF16)
        at = at + dot(slot.astype(BF16), spread)
        gate_of = gate_of + dot(gate.astype(BF16), spread)
    at_ref[...] = at
    gate_ref[...] = gate_of

    fresh = mine(nl_sc).astype(BF16)
    q_rows = [q_sc[:, r].astype(F32).reshape(per_req, width).astype(BF16) for r in range(reqs)]
    new = dot(jnp.concatenate(q_rows, axis=0), fresh, ((1,), (1,))) * scale
    row = iota(new.shape, 0)
    col = iota(new.shape, 1)
    valid = (row // per_req == col % reqs) & (col // reqs <= (row // heads) % steps)
    new = jnp.where(valid, new, -jnp.inf)
    moves["cache"].wait()
    position = iota((per_req, ctx), 1)
    old = []
    for r in range(reqs):
        score = dot(q_rows[r], cache_sc[r]) * scale
        old.append(jnp.where(position < len_sc[pool * reqs + r], score, -jnp.inf))
    old = jnp.concatenate(old, axis=0)
    top = jnp.maximum(jnp.max(old, axis=1, keepdims=True), jnp.max(new, axis=1, keepdims=True))
    old = jnp.exp(old - top)
    new = jnp.exp(new - top)
    total = jnp.sum(old, axis=1, keepdims=True) + jnp.sum(new, axis=1, keepdims=True)
    old = old.astype(BF16)
    latent = jnp.concatenate(
        [
            dot(old[r * per_req : (r + 1) * per_req], cache_sc[r, :LAT, :], ((1,), (1,)))
            for r in range(reqs)
        ],
        axis=0,
    )
    latent = latent + dot(new.astype(BF16), fresh[:, :LAT])
    latent = latent / total
    for i in range(lat_sc.shape[0]):
        lat_sc[i] = latent[:, i * 128 : (i + 1) * 128]
    moves["uv"].wait()
    head_out = []
    for h in range(heads):
        rows = [
            jnp.concatenate(
                [lat_sc[i, pl.ds(s * heads + h, reqs, stride=per_req), :] for i in range(lat_sc.shape[0])],
                axis=1,
            )
            for s in range(steps)
        ]
        lat_h = jnp.concatenate(rows, axis=0).astype(BF16)
        head_out.append(dot(lat_h, uv_sc[h]).astype(BF16))
    head_out = jnp.concatenate(head_out, axis=1)
    for name in ("hid", "gain", "ow"):
        moves[name].wait()
    mixed = mine(hid_sc) + dot(head_out, ow_sc[...])
    mixed_ref[...] = mixed
    normed = (
        mixed * lax.rsqrt(jnp.mean(mixed * mixed, axis=1, keepdims=True) + 1e-06) * gain_sc[...]
    ).astype(BF16)

    wide = model // parts
    stacked = jnp.concatenate([normed[:, i * wide : (i + 1) * wide] for i in range(parts)], axis=0)
    some = 16
    for e in range(0, experts, some):
        place = (iota((some, ROWS, lanes), 1).astype(F32) == at[e : e + some][:, None, :]).astype(F32)
        place = place.reshape(some * ROWS, lanes).astype(BF16)
        x_ref[e * ROWS : (e + some) * ROWS, :] = dot(place, stacked).astype(BF16)


def attend(pool, lengths, queries, new_latent, cache, hidden_in, gain, uv, ow, ids, gates, capacity):
    steps, demand, heads, width = queries.shape
    reqs = demand // MICRO
    model = hidden_in.shape[2]
    experts = capacity.shape[1]
    tokens = steps * reqs
    parts = ROWS // (CAP * steps)
    lanes = parts * tokens
    outs = [
        jax.ShapeDtypeStruct((experts * ROWS, model // parts), BF16),
        jax.ShapeDtypeStruct((experts, lanes), F32),
        jax.ShapeDtypeStruct((experts, lanes), F32),
        jax.ShapeDtypeStruct((tokens, model), F32),
    ]
    full = lambda a: pl.BlockSpec(a.shape, lambda i, p: (0,) * a.ndim)
    inputs = (lengths, queries, new_latent, cache, hidden_in, gain, uv, ow, ids, gates, capacity)
    like = lambda a: pltpu.VMEM(a.shape, a.dtype)
    return pl.pallas_call(
        attend_kernel,
        out_shape=outs,
        grid_spec=pltpu.PrefetchScalarGridSpec(
            num_scalar_prefetch=1,
            grid=(1,),
            in_specs=[pl.BlockSpec(memory_space=pltpu.HBM)] * len(inputs),
            out_specs=[full(o) for o in outs],
            scratch_shapes=[
                pltpu.SMEM(lengths.shape, lengths.dtype),
                pltpu.VMEM((steps, reqs, heads, width), BF16),
                like(new_latent),
                pltpu.VMEM((reqs,) + cache.shape[1:], BF16),
                like(hidden_in),
                like(gain),
                like(uv),
                like(ow),
                like(ids),
                like(gates),
                like(capacity),
                pltpu.VMEM((LAT // 128, tokens * heads, 128), F32),
                pltpu.SemaphoreType.DMA((len(inputs),)),
            ],
        ),
        compiler_params=pltpu.CompilerParams(vmem_limit_bytes=60 * MIB),
        name="attend",
    )(pool, *inputs)


GROUP = 8


def order_matrix(slots):
    n = GROUP * ROWS
    o, i = iota((n, n), 0), iota((n, n), 1)
    per_part = GROUP * slots
    source = (o % per_part) // slots
    want = source * ROWS + (o // per_part) * slots + o % slots
    return (want == i).astype(BF16)


def serve_kernel(x_ref, gate_up_hbm, down_ref, warm_ref, y_ref, rows_sc, act_sc, y_sc, weight_sc, sem):
    model = rows_sc.shape[1]
    wide = x_ref.shape[1]
    parts = model // wide
    slots = ROWS // parts
    n = GROUP * ROWS
    per_part = GROUP * slots
    groups = x_ref.shape[0] // n
    hidden = down_ref.shape[0]
    block = 256
    columns = [(c, min(block, hidden - c)) for c in range(0, hidden, block)]
    moves = []
    for k, (c, w) in enumerate(columns):
        for i in range(2):
            moves.append(
                pltpu.make_async_copy(
                    gate_up_hbm.at[0, :, pl.ds(i * hidden + c, w)],
                    weight_sc.at[k % 3, :, pl.ds(i * w, w)],
                    sem.at[k % 3, i],
                )
            )

    def begin(k):
        if k < len(columns):
            moves[2 * k].start()
            moves[2 * k + 1].start()

    begin(0)
    begin(1)
    order = order_matrix(slots)
    for g in range(groups):
        got = dot(order, x_ref[g * n : (g + 1) * n, :]).astype(BF16)
        for i in range(parts):
            rows_sc[g * per_part : (g + 1) * per_part, i * wide : (i + 1) * wide] = got[
                i * per_part : (i + 1) * per_part
            ]
    for k, (c, w) in enumerate(columns):
        begin(k + 2)
        moves[2 * k].wait()
        moves[2 * k + 1].wait()
        gate = dot(rows_sc[...], weight_sc[k % 3, :, :w])
        up = dot(rows_sc[...], weight_sc[k % 3, :, w : 2 * w])
        act_sc[:, c : c + w] = (gate / (1.0 + jnp.exp(-gate)) * up).astype(BF16)
    for c in range(0, model, block):
        y_sc[:, c : c + block] = dot(act_sc[...], down_ref[:, c : c + block]).astype(BF16)
    for g in range(groups):
        piece = jnp.concatenate(
            [y_sc[g * per_part : (g + 1) * per_part, i * wide : (i + 1) * wide] for i in range(parts)],
            axis=0,
        )
        y_ref[g * n : (g + 1) * n, :] = dot(order, piece, ((0,), (0,))).astype(BF16)


def serve(x, gate_up, down, warm):
    n_in, wide = x.shape
    _, model, twice = gate_up.shape
    n_rows = n_in * wide // model
    vmem = pl.BlockSpec(memory_space=pltpu.VMEM)
    return pl.pallas_call(
        serve_kernel,
        out_shape=jax.ShapeDtypeStruct((n_in, wide), BF16),
        in_specs=[vmem, pl.BlockSpec(memory_space=pl.ANY), vmem, pl.BlockSpec(memory_space=pl.ANY)],
        out_specs=vmem,
        scratch_shapes=[
            pltpu.VMEM((n_rows, model), BF16),
            pltpu.VMEM((n_rows, twice // 2), BF16),
            pltpu.VMEM((n_rows, model), BF16),
            pltpu.VMEM((3, model, 512), BF16),
            pltpu.SemaphoreType.DMA((3, 2)),
        ],
        compiler_params=pltpu.CompilerParams(vmem_limit_bytes=SERVE_MIB * MIB),
        name="serve",
    )(x, gate_up, down[0], warm)


def combine_kernel(pool_ref, at_ref, gate_ref, y_ref, mixed_ref, keep_ref, give_ref):
    experts, lanes = at_ref.shape
    tokens, model = mixed_ref.shape
    parts = lanes // tokens
    wide = model // parts
    some = 16
    acc = jnp.zeros((lanes, wide), F32)
    for e in range(0, experts, some):
        hit = iota((some, ROWS, lanes), 1).astype(F32) == at_ref[e : e + some][:, None, :]
        weight = jnp.where(hit, gate_ref[e : e + some][:, None, :], 0.0)
        weight = weight.reshape(some * ROWS, lanes).astype(BF16)
        acc = acc + dot(weight, y_ref[e * ROWS : (e + some) * ROWS, :], ((0,), (0,)))
    moe = jnp.concatenate([acc[i * tokens : (i + 1) * tokens] for i in range(parts)], axis=1)
    out = (mixed_ref[...] + moe)
    first, second = out[:, : model // 2], out[:, model // 2 :]
    lower = pool_ref[0] == 0
    keep_ref[...] = jnp.where(lower, first, second).astype(BF16)
    give_ref[...] = jnp.where(lower, second, first).astype(BF16)


def combine(pool, at, gate, y, mixed):
    tokens = mixed.shape[0]
    model = mixed.shape[1]
    full = lambda a: pl.BlockSpec(a.shape, lambda i, p: (0,) * a.ndim)
    half = jax.ShapeDtypeStruct((tokens, model // 2), BF16)
    return pl.pallas_call(
        combine_kernel,
        out_shape=[half, half],
        grid_spec=pltpu.PrefetchScalarGridSpec(
            num_scalar_prefetch=1,
            grid=(1,),
            in_specs=[full(at), full(gate), full(y), pl.BlockSpec((tokens, model), lambda i, p: (0, 0))],
            out_specs=[full(half), full(half)],
        ),
        compiler_params=pltpu.CompilerParams(vmem_limit_bytes=16 * MIB),
        name="combine",
    )(pool, at, gate, y, mixed)


def body(
    queries,
    new_latent,
    cache,
    lengths,
    hidden_in,
    norm_gain,
    uv_weight,
    out_weight,
    expert_ids,
    gate_weight,
    capacity,
    gate_up,
    down,
):
    steps, demand = queries.shape[:2]
    reqs = demand // MICRO
    model = hidden_in.shape[2]
    pool = lax.axis_index("pool")
    pool_arr = jnp.full((1,), pool, jnp.int32)
    ring = [(i, (i + 1) % lax.axis_size("dev")) for i in range(lax.axis_size("dev"))]
    warm = lax.ppermute(new_latent[0, :, :128], "dev", ring)
    x, at, gate, mixed = attend(
        pool_arr, lengths, queries, new_latent, jnp.swapaxes(cache, 1, 2), hidden_in, norm_gain[None, :],
        uv_weight, out_weight, jnp.transpose(expert_ids, (2, 0, 1)), jnp.transpose(gate_weight, (2, 0, 1)),
        capacity[None, :],
    )
    x, warm = lax.optimization_barrier((x, warm))
    trade = functools.partial(
        lax.all_to_all, axis_name="dev", split_axis=0, concat_axis=0, tiled=True
    )
    returned = trade(serve(trade(x), gate_up, down, warm))
    keep, give = combine(pool_arr, at, gate, returned, mixed)
    got = lax.ppermute(give, "pool", [(0, 1), (1, 0)])
    keep = keep.reshape(steps, reqs, model // 2)
    got = got.reshape(steps, reqs, model // 2)
    return jnp.where(
        pool == 0, jnp.concatenate([keep, got], axis=1), jnp.concatenate([got, keep], axis=1)
    )


def solution(mesh):
    in_specs = (
        P(None, "dev", None, None),
        P(None, "dev", None),
        P("dev", None, None),
        P("dev"),
        P(None, "dev", None),
        P(),
        P(),
        P(),
        P(None, "dev", None),
        P(None, "dev", None),
        P(),
        P("dev", None, None),
        P("dev", None, None),
    )
    out_specs = P(None, "dev", "pool")
    return jax.shard_map(body, mesh=mesh, in_specs=in_specs, out_specs=out_specs, check_vma=False)
```

time: 142 us -> 131 us (0.923)
  local copies, waits for them, and re-layouts: 9.56 us -> 0.71 us
  Pallas kernels: 29.9 us -> 26.5 us
  starting transfers between devices: 2.9 us -> 5.36 us
  blocking collectives: 97.1 us -> 95.2 us
    unnamed x21 -> x8, local copies, waits for them, and re-layouts: 9.56 us -> 0.02 us
    pallas_call x1, Pallas kernels: 21.6 us -> 19 us  [serve(): pl.pallas_call(serve_kernel, out_shape=jax.ShapeDtypeStruct((n_in, wide),...]
    ppermute x0 -> x1, starting transfers between devices: none -> 2.47 us  [body(): warm = lax.ppermute(new_latent[0, :, :128], 'dev', ring)]
    all_to_all x2, blocking collectives: 97.1 us -> 95.2 us  [body(): returned = trade(serve(trade(x), gate_up, down, warm))]
  transfers between devices with their start and end apart: 1 -> 2, of which waited for: 1 -> 2; matrix products, arithmetic and copies ran while one was open for 0% -> 0% of each run, Pallas kernels for 0% -> 5%
where the time goes in v1:
time: 131 us; the launch traced here: 130 us
  blocking collectives  95.2 us (73%)
  Pallas kernels  26.5 us (20%)
  starting transfers between devices  5.36 us (4%)
  waiting for transfers between devices  1.87 us (1%)
    all_to_all x2, blocking collectives, body(): returned = trade(serve(trade(x), gate_up, down, warm))  95.2 us
    pallas_call x1, Pallas kernels, serve(): pl.pallas_call(serve_kernel, out_shape=jax.ShapeDtypeStruct((n_in, wide),...  19 us
    pallas_call x1, Pallas kernels, attend(): pl.pallas_call(attend_kernel, out_shape=outs, grid_spec=pltpu.PrefetchSca...  6.78 us
    ppermute x1, starting transfers between devices, body(): got = lax.ppermute(give, 'pool', [(0, 1), (1, 0)])  2.89 us
  transfers between devices with their start and end apart: 2, of which 2 were waited for; matrix products, arithmetic and copies ran while one was open for 0% of the time, Pallas kernels for 5%

profile of v1, /device:TPU:1, one launch (start us, length us, event | category | flops | bytes accessed | tf_op | source)
XLA Modules:
  0.0 130.4 jit_solution(18319449430751690963)
XLA Ops:
  0.0 0.7 slice_bitcast_fusion
  0.7 2.5 %collective-permute-start = (bf16[16,128]{1,0:T(8,128)(2,1)S(1)}, bf16[16,128]{1,0:T(8,128)(2,1)S(1)}, u32[]{:S(2)}, u32[]{:S(2)}) collective-permute-start(bf16[16,128]{1,0:T(8,128)(2,1)S(1)} %slice_bitcast_fusion), channel_id=1, source_target_pairs={{0,1},{1,2},{2,3},{3,4},{4,5},{5,6},{6,7},{7,8},{8,9},{9,10},{10,1... | collective-permute-start | bytes 12296 | tf_op jit(solution)/shard_map/ppermute | solution.py:352
  3.2 6.8 %attend.1 = (bf16[1536,1024]{1,0:T(8,128)(2,1)}, f32[64,64]{1,0:T(8,128)}, f32[64,64]{1,0:T(8,128)}, f32[32,2048]{1,0:T(8,128)}) custom-call(s32[1]{0:T(128)} %bitcast.pool_ref, s32[16]{0:T(128)} %len_hbm.1, bf16[4,16,8,576]{3,2,1,0:T(8,128)(2,1)} %q_hbm.1, bf16[4,16,576]{2,1,0:T(8,128)(2,1)} %nl_hbm.1, bf16[16,576,128]{2,1,0:T(8,128)(2,1)} %bitcast.21, ...), custom_call_target="tpu_custom_call" | custom-call | tf_op jit(solution)/shard_map/attend/pallas_call | solution.py:176
  9.9 1.0 collective-permute-done.warm_ref
  10.9 0.0 copy-start
  10.9 49.0 %all_to_all.22 = bf16[64,24,1024]{2,1,0:T(8,128)(2,1)S(1)} all-to-all(bf16[64,24,1024]{2,1,0:T(8,128)(2,1)} %bitcast.20), channel_id=1, replica_groups=mesh['pool'=2,'dev'=64] {'dev'}, dimensions={0} | all-to-all | bytes 6291456 | tf_op jit(solution)/shard_map/all_to_all | solution.py:362
  59.9 0.0 copy-done
  59.9 19.0 %serve.1 = bf16[1536,1024]{1,0:T(8,128)(2,1)S(1)} custom-call(bf16[1536,1024]{1,0:T(8,128)(2,1)S(1)} %bitcast.15, bf16[1,2048,2816]{2,1,0:T(8,128)(2,1)} %gate_up_hbm.1, bf16[1408,2048]{1,0:T(8,128)(2,1)S(1)} %bitcast.18, bf16[16,128]{1,0:T(8,128)(2,1)S(1)} %collective-permute-done.warm_ref), custom_call_target="tpu_custom_call" | custom-call | tf_op jit(solution)/shard_map/serve/pallas_call | solution.py:275
  79.0 0.0 copy-start.1
  79.0 0.0 copy-start.2
  79.0 0.0 copy-start.3
  79.0 46.2 %all_to_all.23 = bf16[64,24,1024]{2,1,0:T(8,128)(2,1)S(1)} all-to-all(bf16[64,24,1024]{2,1,0:T(8,128)(2,1)S(1)} %bitcast.16), channel_id=1, replica_groups=mesh['pool'=2,'dev'=64] {'dev'}, dimensions={0} | all-to-all | bytes 6291456 | tf_op jit(solution)/shard_map/all_to_all | solution.py:362
  125.2 0.0 copy-done.1
  125.2 0.0 copy-done.2
  125.2 0.0 copy-done.3
  125.2 0.7 combine.1
  125.9 2.9 %collective-permute-start.1 = (bf16[32,1024]{1,0:T(8,128)(2,1)S(1)}, bf16[32,1024]{1,0:T(8,128)(2,1)S(1)}, u32[]{:S(2)}, u32[]{:S(2)}) collective-permute-start(bf16[32,1024]{1,0:T(8,128)(2,1)S(1)} %get-tuple-element.20), channel_id=1, source_target_pairs={{0,64},{64,0},{1,65},{65,1},{2,66},{66,2},{3,67},{67,3},{4,68},{68... | collective-permute-start | bytes 196616 | tf_op jit(solution)/shard_map/ppermute | solution.py:364
  128.8 0.9 collective-permute-done.1
  129.7 0.7 maximum_select_fusion
Async XLA Ops:
  0.7 10.2 %collective-permute-start = (bf16[16,128]{1,0:T(8,128)(2,1)S(1)}, bf16[16,128]{1,0:T(8,128)(2,1)S(1)}, u32[]{:S(2)}, u32[]{:S(2)}) collective-permute-start(bf16[16,128]{1,0:T(8,128)(2,1)S(1)} %slice_bitcast_fusion), channel_id=1, source_target_pairs={{0,1},{1,2},{2,3},{3,4},{4,5},{5,6},{6,7},{7,8},{8,9},{9,10},{10,1... | collective-permute-start | bytes 12296 | tf_op jit(solution)/shard_map/ppermute | solution.py:352
  10.9 49.0 %copy-start = (bf16[1,1408,2048]{2,1,0:T(8,128)(2,1)S(1)}, bf16[1,1408,2048]{2,1,0:T(8,128)(2,1)}, u32[]{:S(2)}) copy-start(bf16[1,1408,2048]{2,1,0:T(8,128)(2,1)} %param.25) | copy-start | bytes 17301508
  79.0 46.2 %copy-start.1 = (f32[32,2048]{1,0:T(8,128)S(1)}, f32[32,2048]{1,0:T(8,128)}, u32[]{:S(2)}) copy-start(f32[32,2048]{1,0:T(8,128)} %get-tuple-element.18.mixed_ref) | copy-start | bytes 786436
  79.0 46.2 %copy-start.2 = (f32[64,64]{1,0:T(8,128)S(1)}, f32[64,64]{1,0:T(8,128)}, u32[]{:S(2)}) copy-start(f32[64,64]{1,0:T(8,128)} %get-tuple-element.13.at_ref) | copy-start | bytes 49156
  79.0 46.2 %copy-start.3 = (f32[64,64]{1,0:T(8,128)S(1)}, f32[64,64]{1,0:T(8,128)}, u32[]{:S(2)}) copy-start(f32[64,64]{1,0:T(8,128)} %get-tuple-element.14.gate_ref) | copy-start | bytes 49156
  125.9 3.8 %collective-permute-start.1 = (bf16[32,1024]{1,0:T(8,128)(2,1)S(1)}, bf16[32,1024]{1,0:T(8,128)(2,1)S(1)}, u32[]{:S(2)}, u32[]{:S(2)}) collective-permute-start(bf16[32,1024]{1,0:T(8,128)(2,1)S(1)} %get-tuple-element.20), channel_id=1, source_target_pairs={{0,64},{64,0},{1,65},{65,1},{2,66},{66,2},{3,67},{67,3},{4,68},{68... | collective-permute-start | bytes 196616 | tf_op jit(solution)/shard_map/ppermute | solution.py:364

commit v2 on v1

--- a/solution.py
+++ b/solution.py
@@ -16,6 +16,7 @@
 F32 = jnp.float32
 BF16 = jnp.bfloat16
 MIB = 1024 * 1024
+ATTEND_MIB = 60
 SERVE_MIB = 40
 
 
@@ -197,7 +198,7 @@
                 pltpu.SemaphoreType.DMA((len(inputs),)),
             ],
         ),
-        compiler_params=pltpu.CompilerParams(vmem_limit_bytes=60 * MIB),
+        compiler_params=pltpu.CompilerParams(vmem_limit_bytes=ATTEND_MIB * MIB),
         name="attend",
     )(pool, *inputs)
 
@@ -214,7 +215,7 @@
     return (want == i).astype(BF16)
 
 
-def serve_kernel(x_ref, gate_up_hbm, down_ref, warm_ref, y_ref, rows_sc, act_sc, y_sc, weight_sc, sem):
+def serve_kernel(x_ref, gate_up_hbm, down_ref, y_ref, rows_sc, act_sc, y_sc, weight_sc, sem):
     model = rows_sc.shape[1]
     wide = x_ref.shape[1]
     parts = model // wide
@@ -250,13 +251,20 @@
             rows_sc[g * per_part : (g + 1) * per_part, i * wide : (i + 1) * wide] = got[
                 i * per_part : (i + 1) * per_part
             ]
+    def activate(c, w, gate, up):
+        act_sc[:, c : c + w] = (gate / (1.0 + jnp.exp(-gate)) * up).astype(BF16)
+
+    last = None
     for k, (c, w) in enumerate(columns):
         begin(k + 2)
         moves[2 * k].wait()
         moves[2 * k + 1].wait()
         gate = dot(rows_sc[...], weight_sc[k % 3, :, :w])
         up = dot(rows_sc[...], weight_sc[k % 3, :, w : 2 * w])
-        act_sc[:, c : c + w] = (gate / (1.0 + jnp.exp(-gate)) * up).astype(BF16)
+        if last is not None:
+            activate(*last)
+        last = (c, w, gate, up)
+    activate(*last)
     for c in range(0, model, block):
         y_sc[:, c : c + block] = dot(act_sc[...], down_ref[:, c : c + block]).astype(BF16)
     for g in range(groups):
@@ -267,7 +275,7 @@
         y_ref[g * n : (g + 1) * n, :] = dot(order, piece, ((0,), (0,))).astype(BF16)
 
 
-def serve(x, gate_up, down, warm):
+def serve(x, gate_up, down):
     n_in, wide = x.shape
     _, model, twice = gate_up.shape
     n_rows = n_in * wide // model
@@ -275,7 +283,7 @@
     return pl.pallas_call(
         serve_kernel,
         out_shape=jax.ShapeDtypeStruct((n_in, wide), BF16),
-        in_specs=[vmem, pl.BlockSpec(memory_space=pl.ANY), vmem, pl.BlockSpec(memory_space=pl.ANY)],
+        in_specs=[vmem, pl.BlockSpec(memory_space=pl.ANY), vmem],
         out_specs=vmem,
         scratch_shapes=[
             pltpu.VMEM((n_rows, model), BF16),
@@ -286,7 +294,7 @@
         ],
         compiler_params=pltpu.CompilerParams(vmem_limit_bytes=SERVE_MIB * MIB),
         name="serve",
-    )(x, gate_up, down[0], warm)
+    )(x, gate_up, down[0])
 
 
 def combine_kernel(pool_ref, at_ref, gate_ref, y_ref, mixed_ref, keep_ref, give_ref):
@@ -348,18 +356,15 @@
     model = hidden_in.shape[2]
     pool = lax.axis_index("pool")
     pool_arr = jnp.full((1,), pool, jnp.int32)
-    ring = [(i, (i + 1) % lax.axis_size("dev")) for i in range(lax.axis_size("dev"))]
-    warm = lax.ppermute(new_latent[0, :, :128], "dev", ring)
     x, at, gate, mixed = attend(
         pool_arr, lengths, queries, new_latent, jnp.swapaxes(cache, 1, 2), hidden_in, norm_gain[None, :],
         uv_weight, out_weight, jnp.transpose(expert_ids, (2, 0, 1)), jnp.transpose(gate_weight, (2, 0, 1)),
         capacity[None, :],
     )
-    x, warm = lax.optimization_barrier((x, warm))
     trade = functools.partial(
         lax.all_to_all, axis_name="dev", split_axis=0, concat_axis=0, tiled=True
     )
-    returned = trade(serve(trade(x), gate_up, down, warm))
+    returned = trade(serve(trade(x), gate_up, down))
     keep, give = combine(pool_arr, at, gate, returned, mixed)
     got = lax.ppermute(give, "pool", [(0, 1), (1, 0)])
     keep = keep.reshape(steps, reqs, model // 2)

time: 131 us -> 129 us (0.985)
  starting transfers between devices: 5.36 us -> 2.91 us
  blocking collectives: 95.2 us -> 97.4 us
    ppermute x1 -> x0, starting transfers between devices: 2.47 us -> none  [body(): warm = lax.ppermute(new_latent[0, :, :128], 'dev', ring)]
    all_to_all x2, blocking collectives: 95.2 us -> 97.4 us  [body(): returned = trade(serve(trade(x), gate_up, down))]
  transfers between devices with their start and end apart: 2 -> 1, of which waited for: 2 -> 1; matrix products, arithmetic and copies ran while one was open for 0% -> 0% of each run, Pallas kernels for 5% -> 0%
where the time goes in v2:
time: 129 us
  blocking collectives  97.4 us (76%)
  Pallas kernels  26.9 us (21%)
  starting transfers between devices  2.91 us (2%)
    all_to_all x2, blocking collectives, body(): returned = trade(serve(trade(x), gate_up, down))  97.4 us
    pallas_call x1, Pallas kernels, serve(): pl.pallas_call(serve_kernel, out_shape=jax.ShapeDtypeStruct((n_in, wide),...  19.4 us
    pallas_call x1, Pallas kernels, attend(): pl.pallas_call(attend_kernel, out_shape=outs, grid_spec=pltpu.PrefetchSca...  6.79 us
    ppermute x1, starting transfers between devices, body(): got = lax.ppermute(give, 'pool', [(0, 1), (1, 0)])  2.91 us
  transfers between devices with their start and end apart: 1, of which 1 were waited for; matrix products, arithmetic and copies ran while one was open for 0% of the time, Pallas kernels for 0%

profile of v2, /device:TPU:1, one launch (start us, length us, event | category | flops | bytes accessed | tf_op | source)
XLA Modules:
  0.0 128.9 jit_solution(10384642696261021871)
XLA Ops:
  0.0 6.8 %attend.1 = (bf16[1536,1024]{1,0:T(8,128)(2,1)}, f32[64,64]{1,0:T(8,128)}, f32[64,64]{1,0:T(8,128)}, f32[32,2048]{1,0:T(8,128)}) custom-call(s32[1]{0:T(128)} %bitcast.pool_ref, s32[16]{0:T(128)} %len_hbm.1, bf16[4,16,8,576]{3,2,1,0:T(8,128)(2,1)} %q_hbm.1, bf16[4,16,576]{2,1,0:T(8,128)(2,1)} %nl_hbm.1, bf16[16,576,128]{2,1,0:T(8,128)(2,1)} %bitcast.19, ...), custom_call_target="tpu_custom_call" | custom-call | tf_op jit(solution)/shard_map/attend/pallas_call | solution.py:177
  6.8 0.0 copy-start
  6.8 51.3 %all_to_all.22 = bf16[64,24,1024]{2,1,0:T(8,128)(2,1)S(1)} all-to-all(bf16[64,24,1024]{2,1,0:T(8,128)(2,1)} %bitcast.18), channel_id=1, replica_groups=mesh['pool'=2,'dev'=64] {'dev'}, dimensions={0} | all-to-all | bytes 6291456 | tf_op jit(solution)/shard_map/all_to_all | solution.py:367
  58.1 0.0 copy-done
  58.1 19.4 %serve.1 = bf16[1536,1024]{1,0:T(8,128)(2,1)S(1)} custom-call(bf16[1536,1024]{1,0:T(8,128)(2,1)S(1)} %bitcast.14, bf16[1,2048,2816]{2,1,0:T(8,128)(2,1)} %gate_up_hbm.1, bf16[1408,2048]{1,0:T(8,128)(2,1)S(1)} %bitcast.16), custom_call_target="tpu_custom_call" | custom-call | tf_op jit(solution)/shard_map/serve/pallas_call | solution.py:283
  77.5 0.0 copy-start.1
  77.5 0.0 copy-start.2
  77.5 0.0 copy-start.3
  77.6 46.1 %all_to_all.23 = bf16[64,24,1024]{2,1,0:T(8,128)(2,1)S(1)} all-to-all(bf16[64,24,1024]{2,1,0:T(8,128)(2,1)S(1)} %bitcast.15), channel_id=1, replica_groups=mesh['pool'=2,'dev'=64] {'dev'}, dimensions={0} | all-to-all | bytes 6291456 | tf_op jit(solution)/shard_map/all_to_all | solution.py:367
  123.7 0.0 copy-done.1
  123.7 0.0 copy-done.2
  123.7 0.0 copy-done.3
  123.7 0.7 combine.1
  124.4 2.9 %collective-permute-start = (bf16[32,1024]{1,0:T(8,128)(2,1)S(1)}, bf16[32,1024]{1,0:T(8,128)(2,1)S(1)}, u32[]{:S(2)}, u32[]{:S(2)}) collective-permute-start(bf16[32,1024]{1,0:T(8,128)(2,1)S(1)} %get-tuple-element.16), channel_id=1, source_target_pairs={{0,64},{64,0},{1,65},{65,1},{2,66},{66,2},{3,67},{67,3},{4,68},{68... | collective-permute-start | bytes 196616 | tf_op jit(solution)/shard_map/ppermute | solution.py:369
  127.3 0.9 collective-permute-done
  128.2 0.7 maximum_select_fusion
Async XLA Ops:
  6.8 51.3 %copy-start = (bf16[1,1408,2048]{2,1,0:T(8,128)(2,1)S(1)}, bf16[1,1408,2048]{2,1,0:T(8,128)(2,1)}, u32[]{:S(2)}) copy-start(bf16[1,1408,2048]{2,1,0:T(8,128)(2,1)} %param.25) | copy-start | bytes 17301508
  77.5 46.1 %copy-start.1 = (f32[32,2048]{1,0:T(8,128)S(1)}, f32[32,2048]{1,0:T(8,128)}, u32[]{:S(2)}) copy-start(f32[32,2048]{1,0:T(8,128)} %get-tuple-element.14.mixed_ref) | copy-start | bytes 786436
  77.5 46.1 %copy-start.2 = (f32[64,64]{1,0:T(8,128)S(1)}, f32[64,64]{1,0:T(8,128)}, u32[]{:S(2)}) copy-start(f32[64,64]{1,0:T(8,128)} %get-tuple-element.11.at_ref) | copy-start | bytes 49156
  77.5 46.1 %copy-start.3 = (f32[64,64]{1,0:T(8,128)S(1)}, f32[64,64]{1,0:T(8,128)}, u32[]{:S(2)}) copy-start(f32[64,64]{1,0:T(8,128)} %get-tuple-element.12.gate_ref) | copy-start | bytes 49156
  124.4 3.8 %collective-permute-start = (bf16[32,1024]{1,0:T(8,128)(2,1)S(1)}, bf16[32,1024]{1,0:T(8,128)(2,1)S(1)}, u32[]{:S(2)}, u32[]{:S(2)}) collective-permute-start(bf16[32,1024]{1,0:T(8,128)(2,1)S(1)} %get-tuple-element.16), channel_id=1, source_target_pairs={{0,64},{64,0},{1,65},{65,1},{2,66},{66,2},{3,67},{67,3},{4,68},{68... | collective-permute-start | bytes 196616 | tf_op jit(solution)/shard_map/ppermute | solution.py:369

commit v3 on v2

--- a/solution.py
+++ b/solution.py
@@ -16,8 +16,8 @@
 F32 = jnp.float32
 BF16 = jnp.bfloat16
 MIB = 1024 * 1024
-ATTEND_MIB = 60
-SERVE_MIB = 40
+ATTEND_MIB = 40
+SERVE_MIB = 31
 
 
 def iota(shape, dim):
@@ -173,6 +173,7 @@
     ]
     full = lambda a: pl.BlockSpec(a.shape, lambda i, p: (0,) * a.ndim)
     inputs = (lengths, queries, new_latent, cache, hidden_in, gain, uv, ow, ids, gates, capacity)
+    inputs = tuple(pltpu.with_memory_space_constraint(a, pltpu.HBM) for a in inputs)
     like = lambda a: pltpu.VMEM(a.shape, a.dtype)
     return pl.pallas_call(
         attend_kernel,
@@ -215,7 +216,7 @@
     return (want == i).astype(BF16)
 
 
-def serve_kernel(x_ref, gate_up_hbm, down_ref, y_ref, rows_sc, act_sc, y_sc, weight_sc, sem):
+def serve_kernel(x_ref, gate_up_ref, down_hbm, y_ref, rows_sc, act_sc, down_sc, sem):
     model = rows_sc.shape[1]
     wide = x_ref.shape[1]
     parts = model // wide
@@ -223,27 +224,9 @@
     n = GROUP * ROWS
     per_part = GROUP * slots
     groups = x_ref.shape[0] // n
-    hidden = down_ref.shape[0]
-    block = 256
-    columns = [(c, min(block, hidden - c)) for c in range(0, hidden, block)]
-    moves = []
-    for k, (c, w) in enumerate(columns):
-        for i in range(2):
-            moves.append(
-                pltpu.make_async_copy(
-                    gate_up_hbm.at[0, :, pl.ds(i * hidden + c, w)],
-                    weight_sc.at[k % 3, :, pl.ds(i * w, w)],
-                    sem.at[k % 3, i],
-                )
-            )
-
-    def begin(k):
-        if k < len(columns):
-            moves[2 * k].start()
-            moves[2 * k + 1].start()
-
-    begin(0)
-    begin(1)
+    hidden = down_hbm.shape[0]
+    fetch = pltpu.make_async_copy(down_hbm, down_sc, sem)
+    fetch.start()
     order = order_matrix(slots)
     for g in range(groups):
         got = dot(order, x_ref[g * n : (g + 1) * n, :]).astype(BF16)
@@ -251,25 +234,18 @@
             rows_sc[g * per_part : (g + 1) * per_part, i * wide : (i + 1) * wide] = got[
                 i * per_part : (i + 1) * per_part
             ]
-    def activate(c, w, gate, up):
+    block = 256
+    for c in range(0, hidden, block):
+        w = min(block, hidden - c)
+        gate = dot(rows_sc[...], gate_up_ref[0, :, c : c + w])
+        up = dot(rows_sc[...], gate_up_ref[0, :, hidden + c : hidden + c + w])
         act_sc[:, c : c + w] = (gate / (1.0 + jnp.exp(-gate)) * up).astype(BF16)
-
-    last = None
-    for k, (c, w) in enumerate(columns):
-        begin(k + 2)
-        moves[2 * k].wait()
-        moves[2 * k + 1].wait()
-        gate = dot(rows_sc[...], weight_sc[k % 3, :, :w])
-        up = dot(rows_sc[...], weight_sc[k % 3, :, w : 2 * w])
-        if last is not None:
-            activate(*last)
-        last = (c, w, gate, up)
-    activate(*last)
+    fetch.wait()
     for c in range(0, model, block):
-        y_sc[:, c : c + block] = dot(act_sc[...], down_ref[:, c : c + block]).astype(BF16)
+        rows_sc[:, c : c + block] = dot(act_sc[...], down_sc[:, c : c + block]).astype(BF16)
     for g in range(groups):
         piece = jnp.concatenate(
-            [y_sc[g * per_part : (g + 1) * per_part, i * wide : (i + 1) * wide] for i in range(parts)],
+            [rows_sc[g * per_part : (g + 1) * per_part, i * wide : (i + 1) * wide] for i in range(parts)],
             axis=0,
         )
         y_ref[g * n : (g + 1) * n, :] = dot(order, piece, ((0,), (0,))).astype(BF16)
@@ -283,18 +259,17 @@
     return pl.pallas_call(
         serve_kernel,
         out_shape=jax.ShapeDtypeStruct((n_in, wide), BF16),
-        in_specs=[vmem, pl.BlockSpec(memory_space=pl.ANY), vmem],
+        in_specs=[vmem, vmem, pl.BlockSpec(memory_space=pl.ANY)],
         out_specs=vmem,
         scratch_shapes=[
             pltpu.VMEM((n_rows, model), BF16),
             pltpu.VMEM((n_rows, twice // 2), BF16),
-            pltpu.VMEM((n_rows, model), BF16),
-            pltpu.VMEM((3, model, 512), BF16),
-            pltpu.SemaphoreType.DMA((3, 2)),
+            pltpu.VMEM(down.shape[1:], BF16),
+            pltpu.SemaphoreType.DMA,
         ],
         compiler_params=pltpu.CompilerParams(vmem_limit_bytes=SERVE_MIB * MIB),
         name="serve",
-    )(x, gate_up, down[0])
+    )(x, gate_up, pltpu.with_memory_space_constraint(down[0], pltpu.HBM))
 
 
 def combine_kernel(pool_ref, at_ref, gate_ref, y_ref, mixed_ref, keep_ref, give_ref):

time: 129 us -> 126 us (0.977)
  Pallas kernels: 26.9 us -> 24.8 us
    pallas_call x1, Pallas kernels: 6.79 us -> 5.25 us  [attend(): pl.pallas_call(attend_kernel, out_shape=outs, grid_spec=pltpu.PrefetchSca...]
where the time goes in v3:
time: 126 us
  blocking collectives  96.9 us (77%)
  Pallas kernels  24.8 us (20%)
  starting transfers between devices  2.9 us (2%)
    all_to_all x2, blocking collectives, body(): returned = trade(serve(trade(x), gate_up, down))  96.9 us
    pallas_call x1, Pallas kernels, serve(): pl.pallas_call(serve_kernel, out_shape=jax.ShapeDtypeStruct((n_in, wide),...  18.9 us
    pallas_call x1, Pallas kernels, attend(): pl.pallas_call(attend_kernel, out_shape=outs, grid_spec=pltpu.PrefetchSca...  5.25 us
    ppermute x1, starting transfers between devices, body(): got = lax.ppermute(give, 'pool', [(0, 1), (1, 0)])  2.9 us
  transfers between devices with their start and end apart: 1, of which 1 were waited for; matrix products, arithmetic and copies ran while one was open for 0% of the time, Pallas kernels for 0%

profile of v3, /device:TPU:1, one launch (start us, length us, event | category | flops | bytes accessed | tf_op | source)
XLA Modules:
  0.0 126.2 jit_solution(7259667297376801158)
XLA Ops:
  0.0 0.0 copy-start
  0.0 5.2 %attend.1 = (bf16[1536,1024]{1,0:T(8,128)(2,1)S(1)}, f32[64,64]{1,0:T(8,128)S(1)}, f32[64,64]{1,0:T(8,128)S(1)}, f32[32,2048]{1,0:T(8,128)S(1)}) custom-call(s32[1]{0:T(128)} %bitcast.pool_ref, s32[16]{0:T(128)} %len_hbm.1, bf16[4,16,8,576]{3,2,1,0:T(8,128)(2,1)} %q_hbm.1, bf16[4,16,576]{2,1,0:T(8,128)(2,1)} %nl_hbm.1, bf16[16,576,128]{2,1,0:T(8,128)(2,1)} %bitcast.19, ...), custom_call_target="tpu_custom_call" | custom-call | tf_op jit(solution)/shard_map/attend/pallas_call | solution.py:178
  5.3 51.0 %all_to_all.22 = bf16[64,24,1024]{2,1,0:T(8,128)(2,1)S(1)} all-to-all(bf16[64,24,1024]{2,1,0:T(8,128)(2,1)S(1)} %bitcast.16), channel_id=1, replica_groups=mesh['pool'=2,'dev'=64] {'dev'}, dimensions={0} | all-to-all | bytes 6291456 | tf_op jit(solution)/shard_map/all_to_all | solution.py:342
  56.2 0.0 copy-done
  56.2 18.9 %serve.1 = bf16[1536,1024]{1,0:T(8,128)(2,1)S(1)} custom-call(bf16[1536,1024]{1,0:T(8,128)(2,1)S(1)} %bitcast.14, bf16[1,2048,2816]{2,1,0:T(8,128)(2,1)S(1)} %copy-done, bf16[1408,2048]{1,0:T(8,128)(2,1)} %bitcast.18), custom_call_target="tpu_custom_call" | custom-call | tf_op jit(solution)/shard_map/serve/pallas_call | solution.py:259
  75.1 46.0 %all_to_all.23 = bf16[64,24,1024]{2,1,0:T(8,128)(2,1)S(1)} all-to-all(bf16[64,24,1024]{2,1,0:T(8,128)(2,1)S(1)} %bitcast.15), channel_id=1, replica_groups=mesh['pool'=2,'dev'=64] {'dev'}, dimensions={0} | all-to-all | bytes 6291456 | tf_op jit(solution)/shard_map/all_to_all | solution.py:342
  121.1 0.7 combine.1
  121.8 2.9 %collective-permute-start = (bf16[32,1024]{1,0:T(8,128)(2,1)S(1)}, bf16[32,1024]{1,0:T(8,128)(2,1)S(1)}, u32[]{:S(2)}, u32[]{:S(2)}) collective-permute-start(bf16[32,1024]{1,0:T(8,128)(2,1)S(1)} %get-tuple-element.16), channel_id=1, source_target_pairs={{0,64},{64,0},{1,65},{65,1},{2,66},{66,2},{3,67},{67,3},{4,68},{68... | collective-permute-start | bytes 196616 | tf_op jit(solution)/shard_map/ppermute | solution.py:344
  124.7 0.9 collective-permute-done
  125.6 0.7 maximum_select_fusion
Async XLA Ops:
  0.0 56.2 %copy-start = (bf16[1,2048,2816]{2,1,0:T(8,128)(2,1)S(1)}, bf16[1,2048,2816]{2,1,0:T(8,128)(2,1)}, u32[]{:S(2)}) copy-start(bf16[1,2048,2816]{2,1,0:T(8,128)(2,1)} %gate_up_ref.1) | copy-start | bytes 34603012
  121.8 3.8 %collective-permute-start = (bf16[32,1024]{1,0:T(8,128)(2,1)S(1)}, bf16[32,1024]{1,0:T(8,128)(2,1)S(1)}, u32[]{:S(2)}, u32[]{:S(2)}) collective-permute-start(bf16[32,1024]{1,0:T(8,128)(2,1)S(1)} %get-tuple-element.16), channel_id=1, source_target_pairs={{0,64},{64,0},{1,65},{65,1},{2,66},{66,2},{3,67},{67,3},{4,68},{68... | collective-permute-start | bytes 196616 | tf_op jit(solution)/shard_map/ppermute | solution.py:344

commit v4 on v3

--- a/solution.py
+++ b/solution.py
@@ -171,34 +171,29 @@
         jax.ShapeDtypeStruct((experts, lanes), F32),
         jax.ShapeDtypeStruct((tokens, model), F32),
     ]
-    full = lambda a: pl.BlockSpec(a.shape, lambda i, p: (0,) * a.ndim)
     inputs = (lengths, queries, new_latent, cache, hidden_in, gain, uv, ow, ids, gates, capacity)
     inputs = tuple(pltpu.with_memory_space_constraint(a, pltpu.HBM) for a in inputs)
     like = lambda a: pltpu.VMEM(a.shape, a.dtype)
     return pl.pallas_call(
         attend_kernel,
         out_shape=outs,
-        grid_spec=pltpu.PrefetchScalarGridSpec(
-            num_scalar_prefetch=1,
-            grid=(1,),
-            in_specs=[pl.BlockSpec(memory_space=pltpu.HBM)] * len(inputs),
-            out_specs=[full(o) for o in outs],
-            scratch_shapes=[
-                pltpu.SMEM(lengths.shape, lengths.dtype),
-                pltpu.VMEM((steps, reqs, heads, width), BF16),
-                like(new_latent),
-                pltpu.VMEM((reqs,) + cache.shape[1:], BF16),
-                like(hidden_in),
-                like(gain),
-                like(uv),
-                like(ow),
-                like(ids),
-                like(gates),
-                like(capacity),
-                pltpu.VMEM((LAT // 128, tokens * heads, 128), F32),
-                pltpu.SemaphoreType.DMA((len(inputs),)),
-            ],
-        ),
+        in_specs=[pl.BlockSpec(memory_space=pltpu.SMEM)] + [pl.BlockSpec(memory_space=pltpu.HBM)] * len(inputs),
+        out_specs=[pl.BlockSpec(memory_space=pltpu.VMEM)] * len(outs),
+        scratch_shapes=[
+            pltpu.SMEM(lengths.shape, lengths.dtype),
+            pltpu.VMEM((steps, reqs, heads, width), BF16),
+            like(new_latent),
+            pltpu.VMEM((reqs,) + cache.shape[1:], BF16),
+            like(hidden_in),
+            like(gain),
+            like(uv),
+            like(ow),
+            like(ids),
+            like(gates),
+            like(capacity),
+            pltpu.VMEM((LAT // 128, tokens * heads, 128), F32),
+            pltpu.SemaphoreType.DMA((len(inputs),)),
+        ],
         compiler_params=pltpu.CompilerParams(vmem_limit_bytes=ATTEND_MIB * MIB),
         name="attend",
     )(pool, *inputs)

time: 126 us -> 126 us (level)
  no operation moved by 1% of the time
where the time goes in v4:
time: 126 us
  blocking collectives  96.9 us (77%)
  Pallas kernels  24.8 us (20%)
  starting transfers between devices  2.9 us (2%)
    all_to_all x2, blocking collectives, body(): returned = trade(serve(trade(x), gate_up, down))  96.9 us
    pallas_call x1, Pallas kernels, serve(): pl.pallas_call(serve_kernel, out_shape=jax.ShapeDtypeStruct((n_in, wide),...  18.9 us
    pallas_call x1, Pallas kernels, attend(): pl.pallas_call(attend_kernel, out_shape=outs, in_specs=[pl.BlockSpec(memo...  5.25 us
    ppermute x1, starting transfers between devices, body(): got = lax.ppermute(give, 'pool', [(0, 1), (1, 0)])  2.9 us
  transfers between devices with their start and end apart: 1, of which 1 were waited for; matrix products, arithmetic and copies ran while one was open for 0% of the time, Pallas kernels for 0%

profile of v4, /device:TPU:1, one launch (start us, length us, event | category | flops | bytes accessed | tf_op | source)
XLA Modules:
  0.0 126.2 jit_solution(7259667297376801158)
XLA Ops:
  0.0 0.0 copy-start
  0.0 5.2 %attend.1 = (bf16[1536,1024]{1,0:T(8,128)(2,1)S(1)}, f32[64,64]{1,0:T(8,128)S(1)}, f32[64,64]{1,0:T(8,128)S(1)}, f32[32,2048]{1,0:T(8,128)S(1)}) custom-call(s32[1]{0:T(128)} %bitcast.pool_ref, s32[16]{0:T(128)} %len_hbm.1, bf16[4,16,8,576]{3,2,1,0:T(8,128)(2,1)} %q_hbm.1, bf16[4,16,576]{2,1,0:T(8,128)(2,1)} %nl_hbm.1, bf16[16,576,128]{2,1,0:T(8,128)(2,1)} %bitcast.19, ...), custom_call_target="tpu_custom_call" | custom-call | tf_op jit(solution)/shard_map/attend/pallas_call | solution.py:177
  5.3 51.0 %all_to_all.22 = bf16[64,24,1024]{2,1,0:T(8,128)(2,1)S(1)} all-to-all(bf16[64,24,1024]{2,1,0:T(8,128)(2,1)S(1)} %bitcast.16), channel_id=1, replica_groups=mesh['pool'=2,'dev'=64] {'dev'}, dimensions={0} | all-to-all | bytes 6291456 | tf_op jit(solution)/shard_map/all_to_all | solution.py:337
  56.2 0.0 copy-done
  56.2 18.9 %serve.1 = bf16[1536,1024]{1,0:T(8,128)(2,1)S(1)} custom-call(bf16[1536,1024]{1,0:T(8,128)(2,1)S(1)} %bitcast.14, bf16[1,2048,2816]{2,1,0:T(8,128)(2,1)S(1)} %copy-done, bf16[1408,2048]{1,0:T(8,128)(2,1)} %bitcast.18), custom_call_target="tpu_custom_call" | custom-call | tf_op jit(solution)/shard_map/serve/pallas_call | solution.py:254
  75.1 46.0 %all_to_all.23 = bf16[64,24,1024]{2,1,0:T(8,128)(2,1)S(1)} all-to-all(bf16[64,24,1024]{2,1,0:T(8,128)(2,1)S(1)} %bitcast.15), channel_id=1, replica_groups=mesh['pool'=2,'dev'=64] {'dev'}, dimensions={0} | all-to-all | bytes 6291456 | tf_op jit(solution)/shard_map/all_to_all | solution.py:337
  121.1 0.7 combine.1
  121.8 2.9 %collective-permute-start = (bf16[32,1024]{1,0:T(8,128)(2,1)S(1)}, bf16[32,1024]{1,0:T(8,128)(2,1)S(1)}, u32[]{:S(2)}, u32[]{:S(2)}) collective-permute-start(bf16[32,1024]{1,0:T(8,128)(2,1)S(1)} %get-tuple-element.16), channel_id=1, source_target_pairs={{0,64},{64,0},{1,65},{65,1},{2,66},{66,2},{3,67},{67,3},{4,68},{68... | collective-permute-start | bytes 196616 | tf_op jit(solution)/shard_map/ppermute | solution.py:339
  124.7 0.9 collective-permute-done
  125.6 0.7 maximum_select_fusion
Async XLA Ops:
  0.0 56.2 %copy-start = (bf16[1,2048,2816]{2,1,0:T(8,128)(2,1)S(1)}, bf16[1,2048,2816]{2,1,0:T(8,128)(2,1)}, u32[]{:S(2)}) copy-start(bf16[1,2048,2816]{2,1,0:T(8,128)(2,1)} %gate_up_ref.1) | copy-start | bytes 34603012
  121.8 3.8 %collective-permute-start = (bf16[32,1024]{1,0:T(8,128)(2,1)S(1)}, bf16[32,1024]{1,0:T(8,128)(2,1)S(1)}, u32[]{:S(2)}, u32[]{:S(2)}) collective-permute-start(bf16[32,1024]{1,0:T(8,128)(2,1)S(1)} %get-tuple-element.16), channel_id=1, source_target_pairs={{0,64},{64,0},{1,65},{65,1},{2,66},{66,2},{3,67},{67,3},{4,68},{68... | collective-permute-start | bytes 196616 | tf_op jit(solution)/shard_map/ppermute | solution.py:339
